TPU v7x, 32 devices: a whole 2x2x4 slice. The times are simulated.
32 devices in a mesh: groups: 2 (over x), inst: 4 (over z), dp: 4 (over y, core).
Axes of the slice: x: 2, y: 2, z: 4, core: 2. Of those that a mesh axis runs over, the one named last changes fastest.
Arguments:
- hidden: bfloat16 [16384, 7168], P(('groups', 'inst', 'dp')), parts along dimension 0, may hold values from -6 to 6
- input_gain: float32 [7168], replicated, may hold values from 0.1 to 1.9
- w_latent: bfloat16 [7168, 576], replicated, may hold values from -0.0625 to 0.0625
- latent_norm_gain: float32 [512], replicated, may hold values from 0.1 to 1.9
- req_len: int32 [8, 4, 4], P(('groups', 'inst'), 'dp'), parts along dimension 0, may hold values from 1 to 256, 512 in all within a row
- req_dest: int32 [8, 4, 4], P(('groups', 'inst'), 'dp'), parts along dimension 0, may hold values from 0 to 3, as said below
- req_block: int32 [8, 4, 4], P(('groups', 'inst'), 'dp'), parts along dimension 0, may hold values from 0 to 12, as said below
Outputs:
- decode_cache: bfloat16 [32768, 576], P(('groups', 'inst', 'dp')), parts along dimension 0
There are 2 independent parts, one for each index of `groups`. A program takes and returns all parts, laid end to end along the dimension named above; an argument that names none is the same for every part. Nothing has to cross between parts.
Inputs may be any that keep to these rules, and one draw needn't show every extreme that they name: For each rank (i, d), req_dest[i, d, :] is a permutation of the 4 ranks. `req_block`: each is a multiple of 4; the requests that reach one decode device have different pages.
All inputs are finite; a program needn't handle non-finite values.
Results may differ from a plain program's by a relative error of at most 0.005.
Values may be sent and summed in bfloat16 or wider, within the bound.
A program may use at most 64 MiB of HBM per device.

v0:
```python
import jax
import jax.numpy as jnp
from jax import lax
from jax.sharding import PartitionSpec as P

BLOCK = 64


def from_behind(block, axis, distance):
    devices = range(lax.axis_size(axis))
    route = [((i - distance) % len(devices), i) for i in devices]
    return lax.ppermute(block, axis, route)


def apply_rotary(rotary, positions):
    half = rotary.shape[-1] // 2
    inverse = 10000.0 ** (-jnp.arange(half, dtype=jnp.float32) / half)
    angle = positions[:, None] * inverse[None, :]
    first = rotary[:, :half]
    second = rotary[:, half:]
    cosine = jnp.cos(angle)
    sine = jnp.sin(angle)
    return jnp.concatenate([first * cosine - second * sine, first * sine + second * cosine], axis=1)


def request_starts(lengths):
    ends = jnp.cumsum(lengths)
    return (ends - lengths, ends)


def make_rows(hidden, input_gain, w_latent, latent_norm_gain, lengths):
    tokens = hidden.shape[0]
    values = hidden.astype(jnp.float32)
    scale = lax.rsqrt(jnp.mean(values * values, axis=1, keepdims=True) + 1e-06)
    normed = (values * scale * input_gain[None, :]).astype(jnp.bfloat16)
    latent_vectors = jnp.dot(normed, w_latent, preferred_element_type=jnp.float32)
    starts, ends = request_starts(lengths)
    rowpos = jnp.arange(tokens, dtype=jnp.int32)
    inside = ((rowpos[:, None] >= starts[None, :]) & (rowpos[:, None] < ends[None, :])).astype(
        jnp.int32
    )
    positions = (rowpos - jnp.sum(inside * starts[None, :], axis=1)).astype(jnp.float32)
    width = latent_norm_gain.shape[0]
    compressed = latent_vectors[:, :width]
    compressed = (
        compressed
        * lax.rsqrt(jnp.mean(compressed * compressed, axis=1, keepdims=True) + 1e-06)
        * latent_norm_gain[None, :]
    )
    return jnp.concatenate(
        [compressed, apply_rotary(latent_vectors[:, width:], positions)], axis=1
    ).astype(jnp.bfloat16)


def pack_slots(cache_rows_out, lengths, targets, blocks, capacity):
    ranks = lengths.shape[0]
    starts, ends = request_starts(lengths)
    picked = (targets[None, :] == jnp.arange(ranks, dtype=jnp.int32)[:, None]).astype(jnp.int32)
    slot_start = jnp.sum(picked * starts[None, :], axis=1)
    slot_len = jnp.sum(picked * lengths[None, :], axis=1)
    slot_block = jnp.sum(picked * blocks[None, :], axis=1)
    offset = jnp.arange(capacity, dtype=jnp.int32)
    index = jnp.clip(slot_start[:, None] + offset[None, :], 0, cache_rows_out.shape[0] - 1)
    valid = offset[None, :] < slot_len[:, None]
    taken = jnp.take(cache_rows_out, index.reshape(-1), axis=0).reshape(
        ranks, capacity, cache_rows_out.shape[1]
    )
    slots = jnp.where(valid[:, :, None], taken, jnp.zeros_like(taken))
    return (slots, slot_len, slot_block)


def place_slots(slots, slot_len, slot_block, capacity):
    ranks = slots.shape[0]
    reserved = (capacity + BLOCK - 1) // BLOCK
    span = reserved * BLOCK
    groups = jnp.arange(ranks, dtype=jnp.int32)
    owner = (slot_block[None, :] == groups[:, None] * reserved).astype(jnp.int32)
    owner_slot = jnp.sum(owner * groups[None, :], axis=1)
    owner_len = jnp.sum(owner * slot_len[None, :], axis=1)
    within = jnp.arange(span, dtype=jnp.int32)
    index = owner_slot[:, None] * capacity + jnp.minimum(within[None, :], capacity - 1)
    valid = within[None, :] < owner_len[:, None]
    flat = slots.reshape(ranks * capacity, slots.shape[2])
    taken = jnp.take(flat, index.reshape(-1), axis=0).reshape(ranks, span, slots.shape[2])
    placed = jnp.where(valid[:, :, None], taken, jnp.zeros_like(taken))
    return placed.reshape(ranks * span, slots.shape[2])


def on_device(hidden, input_gain, w_latent, latent_norm_gain, req_len, req_dest, req_block):
    ranks = lax.axis_size("dp")
    capacity = 2 * hidden.shape[0] // ranks
    lengths = req_len.reshape(ranks)
    targets = req_dest.reshape(ranks)
    blocks = req_block.reshape(ranks)
    cache_rows_out = make_rows(hidden, input_gain, w_latent, latent_norm_gain, lengths)
    partner = lax.axis_size("inst") // 2
    slots, slot_len, slot_block = pack_slots(cache_rows_out, lengths, targets, blocks, capacity)
    slots, slot_len, slot_block = (
        lax.all_to_all(slots, "dp", split_axis=0, concat_axis=0, tiled=True),
        lax.all_to_all(slot_len, "dp", split_axis=0, concat_axis=0, tiled=True),
        lax.all_to_all(slot_block, "dp", split_axis=0, concat_axis=0, tiled=True),
    )
    slots, slot_len, slot_block = from_behind((slots, slot_len, slot_block), "inst", partner)
    return place_slots(slots, slot_len, slot_block, capacity)


def solution(mesh):
    placed = (
        P(("groups", "inst", "dp"), None),
        P(),
        P(),
        P(),
        P(("groups", "inst"), "dp", None),
        P(("groups", "inst"), "dp", None),
        P(("groups", "inst"), "dp", None),
    )
    return jax.shard_map(
        on_device,
        mesh=mesh,
        in_specs=placed,
        out_specs=P(("groups", "inst", "dp"), None),
        check_vma=False,
    )
```

profile of v0, /device:TPU:1, one launch (start us, length us, event | category | flops | bytes accessed | tf_op | source)
XLA Modules:
  0.0 112.5 jit_solution(8657323201282194274)
XLA Ops:
  0.0 0.8 reduce-window.7
  0.8 0.7 bitcast_subtract_fusion
  1.5 0.8 select_reduce_fusion.3
  2.3 0.7 copy.23
  3.0 4.3 %all-to-all-start.1 = ((s32[4,1,1]{2,1,0:T(1,128)}), s32[4,1,1]{2,1,0:T(1,128)S(1)}, u32[]{:S(2)}, u32[]{:S(2)}) async-start(s32[4,1,1]{2,1,0:T(1,128)} %copy.23), calls=%async_computation.1 | async-start | bytes 4096 | tf_op jit(solution)/shard_map/all_to_all | solution.py:100
  7.7 4.7 %fusion = f32[512]{0:T(512)S(1)} fusion(bf16[512,7168]{1,0:T(8,128)(2,1)} %param.7), kind=kLoop, calls=%fused_computation.4 | loop fusion | flops 11009536 | bytes 7342080 | tf_op jit(solution)/shard_map/reduce_sum | solution.py:34
  12.5 0.4 copy-done
  12.8 7.0 %fusion.3 = f32[512,576]{0,1:T(8,128)S(1)} fusion(bf16[7168,576]{0,1:T(8,128)(2,1)} %param.9, bf16[512,7168]{1,0:T(8,128)(2,1)S(1)} %copy-done, f32[7168]{0:T(1024)S(1)} %copy-done.2, f32[512]{0:T(512)S(1)} %add_rsqrt_fusion.1), kind=kOutput, calls=%fused_computation.7 | convolution fusion | flops 4242538496 | bytes 16807936 | tf_op jit(solution)/shard_map/dot_general | solution.py:36
  20.0 0.3 fusion.12
  20.8 4.0 %gather_fusion = bf16[1024,576]{1,0:T(8,128)(2,1)S(1)} fusion(bf16[512,576]{1,0:T(8,128)(2,1)S(1)} %copy.24, s32[1024]{0:T(1024)S(1)} %broadcast_clamp_fusion.1), kind=kCustom, calls=%fused_computation | custom fusion | bytes 2363392 | tf_op jit(solution)/shard_map/jit(_take)/gather | solution.py:65
  24.9 0.6 copy.25
  25.5 1.2 %select_select_fusion.1 = bf16[4,256,576]{1,2,0:T(8,128)(2,1)} fusion(bf16[4,256,576]{1,2,0:T(8,128)(2,1)S(1)} %copy.25, pred[4,256]{1,0:T(4,128)(4,1)S(1)} %get-tuple-element.15, pred[4,256]{1,0:T(4,128)(4,1)S(1)} %get-tuple-element.14), kind=kLoop, calls=%fused_computation.11 | loop fusion | flops 1179648 | bytes 2361344 | tf_op jit(solution)/shard_map/jit(_where)/select_n | solution.py:68
  26.7 6.1 %all_to_all.29 = s32[4,1,1]{2,1,0:T(1,128)S(1)} all-to-all(s32[4,1,1]{2,1,0:T(1,128)S(1)} %copy.22), channel_id=1, replica_groups=mesh['groups'=2,'inst'=4,'dp'=4] {'dp'}, dimensions={0} | all-to-all | bytes 32 | tf_op jit(solution)/shard_map/all_to_all | solution.py:101
  32.8 4.2 %all-to-all-start.2 = ((bf16[4,256,576]{1,2,0:T(8,128)(2,1)}), bf16[4,256,576]{1,2,0:T(8,128)(2,1)S(1)}, u32[]{:S(2)}, u32[]{:S(2)}) async-start(bf16[4,256,576]{1,2,0:T(8,128)(2,1)} %select_select_fusion.1), calls=%async_computation.2 | async-start | bytes 2359296 | tf_op jit(solution)/shard_map/all_to_all | solution.py:99
  37.2 2.8 %collective-permute-start = (s32[4]{0:T(128)S(1)}, s32[4]{0:T(128)S(1)}, u32[]{:S(2)}, u32[]{:S(2)}) collective-permute-start(s32[4]{0:T(128)S(1)} %reduce), channel_id=1, source_target_pairs={{8,0},{12,4},{0,8},{4,12},{9,1},{13,5},{1,9},{5,13},{10,2},{14,6},... | collective-permute-start | bytes 56 | tf_op jit(solution)/shard_map/ppermute | solution.py:12
  40.2 0.7 collective-permute-done
  40.9 2.6 %collective-permute-done.1 = s32[4]{0:T(128)S(1)} collective-permute-done((s32[4]{0:T(128)S(1)}, s32[4]{0:T(128)S(1)}, u32[]{:S(2)}, u32[]{:S(2)}) %collective-permute-start.1) | collective-permute-done | bytes 48 | tf_op jit(solution)/shard_map/ppermute | solution.py:12
  43.7 8.3 %all-to-all-done.2 = bf16[4,256,576]{1,2,0:T(8,128)(2,1)S(1)} async-done(((bf16[4,256,576]{1,2,0:T(8,128)(2,1)}), bf16[4,256,576]{1,2,0:T(8,128)(2,1)S(1)}, u32[]{:S(2)}, u32[]{:S(2)}) %all-to-all-start.2) | async-done | bytes 1179680 | tf_op jit(solution)/shard_map/all_to_all | solution.py:99
  52.0 2.7 %collective-permute-start.2 = (bf16[4,256,576]{1,2,0:T(8,128)(2,1)S(1)}, bf16[4,256,576]{1,2,0:T(8,128)(2,1)S(1)}, u32[]{:S(2)}, u32[]{:S(2)}) collective-permute-start(bf16[4,256,576]{1,2,0:T(8,128)(2,1)S(1)} %all-to-all-done.2), channel_id=1, source_target_pairs={{8,0},{12,4},{0,8},{4,12},{9,1},{13,5},{1,9},{5,13},{10,2},{14,6},... | collective-permute-start | bytes 3538952 | tf_op jit(solution)/shard_map/ppermute | solution.py:12
  55.0 50.5 %collective-permute-done.2 = bf16[4,256,576]{1,2,0:T(8,128)(2,1)S(1)} collective-permute-done((bf16[4,256,576]{1,2,0:T(8,128)(2,1)S(1)}, bf16[4,256,576]{1,2,0:T(8,128)(2,1)S(1)}, u32[]{:S(2)}, u32[]{:S(2)}) %collective-permute-start.2) | collective-permute-done | bytes 1179680 | tf_op jit(solution)/shard_map/ppermute | solution.py:12
  105.5 0.7 copy.26
  106.2 4.0 %gather_fusion.1 = bf16[1024,576]{1,0:T(8,128)(2,1)S(1)} fusion(bf16[1024,576]{1,0:T(8,128)(2,1)S(1)} %bitcast.27, s32[1024]{0:T(1024)S(1)} %broadcast_clamp_fusion), kind=kCustom, calls=%fused_computation.1 | custom fusion | bytes 2363392 | tf_op jit(solution)/shard_map/jit(_take)/gather | solution.py:84
  110.2 0.9 select_select_fusion
  111.1 1.4 %copy.27 = bf16[1024,576]{0,1:T(8,128)(2,1)} copy(bf16[1024,576]{1,0:T(8,128)(2,1)S(1)} %select_select_fusion) | data formatting | bytes 2359296 | tf_op jit(solution)/shard_map/jit(_where)/select_n | solution.py:85
  (36 shorter events, 1.8 us)
Async XLA Ops:
  3.0 23.7 %all-to-all-start.1 = ((s32[4,1,1]{2,1,0:T(1,128)}), s32[4,1,1]{2,1,0:T(1,128)S(1)}, u32[]{:S(2)}, u32[]{:S(2)}) async-start(s32[4,1,1]{2,1,0:T(1,128)} %copy.23), calls=%async_computation.1 | async-start | bytes 4096 | tf_op jit(solution)/shard_map/all_to_all | solution.py:100
  7.7 5.2 %copy-start = (bf16[512,7168]{1,0:T(8,128)(2,1)S(1)}, bf16[512,7168]{1,0:T(8,128)(2,1)}, u32[]{:S(2)}) copy-start(bf16[512,7168]{1,0:T(8,128)(2,1)} %param.7) | copy-start | bytes 22020100
  7.7 5.2 %copy-start.2 = (f32[7168]{0:T(1024)S(1)}, f32[7168]{0:T(1024)}, u32[]{:S(2)}) copy-start(f32[7168]{0:T(1024)} %param.8) | copy-start | bytes 86020
  12.8 7.5 %copy-start.1 = (f32[512]{0:T(512)S(1)}, f32[512]{0:T(512)}, u32[]{:S(2)}) copy-start(f32[512]{0:T(512)} %param.10) | copy-start | bytes 6148
  32.8 19.2 %all-to-all-start.2 = ((bf16[4,256,576]{1,2,0:T(8,128)(2,1)}), bf16[4,256,576]{1,2,0:T(8,128)(2,1)S(1)}, u32[]{:S(2)}, u32[]{:S(2)}) async-start(bf16[4,256,576]{1,2,0:T(8,128)(2,1)} %select_select_fusion.1), calls=%async_computation.2 | async-start | bytes 2359296 | tf_op jit(solution)/shard_map/all_to_all | solution.py:99
  37.2 3.7 %collective-permute-start = (s32[4]{0:T(128)S(1)}, s32[4]{0:T(128)S(1)}, u32[]{:S(2)}, u32[]{:S(2)}) collective-permute-start(s32[4]{0:T(128)S(1)} %reduce), channel_id=1, source_target_pairs={{8,0},{12,4},{0,8},{4,12},{9,1},{13,5},{1,9},{5,13},{10,2},{14,6},... | collective-permute-start | bytes 56 | tf_op jit(solution)/shard_map/ppermute | solution.py:12
  40.1 3.4 %collective-permute-start.1 = (s32[4]{0:T(128)S(1)}, s32[4]{0:T(128)S(1)}, u32[]{:S(2)}, u32[]{:S(2)}) collective-permute-start(s32[4]{0:T(128)S(1)} %reduce.1), channel_id=1, source_target_pairs={{8,0},{12,4},{0,8},{4,12},{9,1},{13,5},{1,9},{5,13},{10,2},{14,6},... | collective-permute-start | bytes 56 | tf_op jit(solution)/shard_map/ppermute | solution.py:12
  52.0 53.5 %collective-permute-start.2 = (bf16[4,256,576]{1,2,0:T(8,128)(2,1)S(1)}, bf16[4,256,576]{1,2,0:T(8,128)(2,1)S(1)}, u32[]{:S(2)}, u32[]{:S(2)}) collective-permute-start(bf16[4,256,576]{1,2,0:T(8,128)(2,1)S(1)} %all-to-all-done.2), channel_id=1, source_target_pairs={{8,0},{12,4},{0,8},{4,12},{9,1},{13,5},{1,9},{5,13},{10,2},{14,6},... | collective-permute-start | bytes 3538952 | tf_op jit(solution)/shard_map/ppermute | solution.py:12
where the time goes:
time: 114 us; the launch traced here: 113 us
  waiting for transfers between devices  62.1 us (54%)
  starting transfers between devices  14.1 us (12%)
  local copies, waits for them, and re-layouts  12.3 us (11%)
  other arithmetic  10.7 us (9%)
  matrix products  7.03 us (6%)
  blocking collectives  6.15 us (5%)
    ppermute x3, waiting for transfers between devices, from_behind(): return lax.ppermute(block, axis, route)  53.8 us
    all_to_all x1, waiting for transfers between devices, on_device(): lax.all_to_all(slots, 'dp', split_axis=0, concat_axis=0, tiled=True)  8.34 us
    dot_general x1, matrix products, make_rows(): jnp.dot(normed, w_latent, preferred_element_type=jnp.float32)  7.03 us
    all_to_all x1, blocking collectives, on_device(): lax.all_to_all(slot_block, 'dp', split_axis=0, concat_axis=0, tiled=True)  6.15 us
    ppermute x3, starting transfers between devices, from_behind(): return lax.ppermute(block, axis, route)  5.61 us
    reduce_sum x1, other arithmetic, make_rows(): scale = lax.rsqrt(jnp.mean(values * values, axis=1, keepdims=True) + 1e-06)  4.75 us
    gather x2, local copies, waits for them, and re-layouts, pack_slots(): jnp.take(cache_rows_out, index.reshape(-1), axis=0)  4.67 us
    all_to_all x1, starting transfers between devices, on_device(): lax.all_to_all(slot_len, 'dp', split_axis=0, concat_axis=0, tiled=True)  4.29 us
  transfers between devices with their start and end apart: 5, of which 4 were waited for; matrix products, arithmetic and copies ran while one was open for 17% of the time, Pallas kernels for 0%

commit v1 on v0

v1 whole, which is shorter than its diff:
```python
import functools
import math

import jax
import jax.numpy as jnp
from jax import lax
from jax.experimental import pallas as pl
from jax.experimental.pallas import tpu as pltpu
from jax.sharding import PartitionSpec as P

BLOCK = 64
LANES = 128
MESH = pl.DeviceIdType.MESH
CHUNKS = (128, 128, 128, 128)
KTILE = 1024


def kernel(
    sizes,
    len_ref,
    dest_ref,
    block_ref,
    gain_ref,
    norm_ref,
    x_ref,
    w_ref,
    out_ref,
    x_v,
    w_v,
    acc,
    trig,
    mine,
    held,
    meta_mine,
    meta_held,
    meta_smem,
    x_sem,
    w_sem,
    z_sem,
    pass_sem,
    relay_sem,
    recv_sem,
    meta_send,
    meta_recv,
    meta_local,
):
    n_inst, n_dp = sizes
    tokens, width = x_v.shape
    latent = norm_ref.shape[1]
    rotary = w_ref.shape[1] - latent
    half = rotary // 2
    pieces = latent // LANES
    capacity = 2 * tokens // n_dp
    n_y = n_dp // 2
    steps = len(CHUNKS)
    first_row = [sum(CHUNKS[:c]) for c in range(steps)]

    def packed(rows):
        return rows * (latent + rotary) // LANES

    group = lax.axis_index("groups")
    inst = lax.axis_index("inst")
    rank = lax.axis_index("dp")
    far = lax.rem(inst + n_inst // 2, n_inst)
    y = rank // 2
    core = lax.rem(rank, 2)
    sibling = y * 2 + 1 - core
    columns = [lax.rem(y + j, n_y) * 2 + core for j in range(1, n_y)]

    w_copies = [
        pltpu.make_async_copy(
            w_ref.at[pl.ds(k * KTILE, KTILE), :], w_v.at[pl.ds(k * KTILE, KTILE), :], w_sem.at[k]
        )
        for k in range(width // KTILE)
    ]
    x_copies = [
        pltpu.make_async_copy(
            x_ref.at[pl.ds(first_row[c], CHUNKS[c]), :],
            x_v.at[pl.ds(first_row[c], CHUNKS[c]), :],
            x_sem.at[c],
        )
        for c in range(steps)
    ]
    x_copies[0].start()
    for copy in w_copies:
        copy.start()
    for copy in x_copies[1:]:
        copy.start()

    barrier = pltpu.get_barrier_semaphore()
    for e in range(n_dp):
        pl.semaphore_signal(barrier, inc=1, device_id=(group, far, e), device_id_type=MESH)
    for other in [sibling] + columns:
        pl.semaphore_signal(barrier, inc=1, device_id=(group, inst, other), device_id_type=MESH)

    starts = []
    total = jnp.int32(0)
    for k in range(n_dp):
        starts.append(total)
        total = total + len_ref[0, 0, k]
    row = lax.broadcasted_iota(jnp.int32, meta_mine.shape, 0)
    lane = lax.broadcasted_iota(jnp.int32, meta_mine.shape, 1)
    table = jnp.zeros(meta_mine.shape, jnp.int32)
    for k in range(n_dp):
        entry = jnp.where(
            lane == 0,
            starts[k],
            jnp.where(lane == 1, len_ref[0, 0, k], block_ref[0, 0, k]),
        )
        table = jnp.where(row == dest_ref[0, 0, k], entry, table)
    meta_mine[...] = table

    turn = lax.broadcasted_iota(jnp.int32, (tokens, LANES), 1)
    which = lax.rem(turn, half).astype(jnp.float32)
    inverse = jnp.exp(which * jnp.float32(-math.log(10000.0) / half))
    at = lax.broadcasted_iota(jnp.int32, (tokens, LANES), 0)
    begin = jnp.zeros((tokens, LANES), jnp.int32)
    for k in range(1, n_dp):
        begin = jnp.where(at >= starts[k], starts[k], begin)
    angle = (at - begin).astype(jnp.float32) * inverse
    angle = jnp.where(turn < rotary, angle, angle - jnp.float32(math.pi / 2))
    trig[...] = jnp.cos(angle)

    def compute(c):
        rows = CHUNKS[c]
        span = pl.ds(first_row[c], rows)
        x_copies[c].wait()
        acc[pl.ds(0, rows), :] = jnp.zeros((rows, acc.shape[1]), jnp.float32)
        squares = jnp.zeros((rows, 1), jnp.float32)
        for k in range(width // KTILE):
            if c == 0:
                w_copies[k].wait()
            cols = pl.ds(k * KTILE, KTILE)
            values = x_v[span, cols].astype(jnp.float32)
            squares = squares + jnp.sum(values * values, axis=1, keepdims=True)
            scaled = (values * gain_ref[:, cols]).astype(jnp.bfloat16)
            acc[pl.ds(0, rows), :] += jnp.dot(
                scaled, w_v[cols, :], preferred_element_type=jnp.float32
            )
        scale = lax.rsqrt(squares * (1.0 / width) + 1e-06)
        compressed = acc[pl.ds(0, rows), pl.ds(0, latent)] * scale
        power = jnp.mean(compressed * compressed, axis=1, keepdims=True)
        compressed = compressed * lax.rsqrt(power + 1e-06) * norm_ref[...]
        compressed = compressed.astype(jnp.bfloat16)
        base = packed(first_row[c])
        for j in range(pieces):
            mine[pl.ds(base + j * rows, rows), :] = compressed[:, j * LANES : (j + 1) * LANES]
        turned = acc[pl.ds(0, rows), pl.ds(latent, rotary)] * scale
        a, b = turned[:, :half], turned[:, half:]
        cosine = trig[span, pl.ds(0, half)]
        sine = trig[span, pl.ds(rotary, half)]
        turned = jnp.concatenate([a * cosine - b * sine, a * sine + b * cosine], axis=1)
        turned = jnp.concatenate([turned[: rows // 2], turned[rows // 2 :]], axis=1)
        mine[pl.ds(base + pieces * rows, rows // 2), :] = turned.astype(jnp.bfloat16)

    def chunk_of(c):
        return pl.ds(packed(first_row[c]), packed(CHUNKS[c]))

    def send_far(c):
        return pltpu.make_async_remote_copy(
            src_ref=mine.at[chunk_of(c)],
            dst_ref=held.at[rank, chunk_of(c)],
            send_sem=z_sem.at[c],
            recv_sem=recv_sem.at[rank, c],
            device_id=(group, far, rank),
            device_id_type=MESH,
        )

    def pass_on(c, source, target, sem):
        return pltpu.make_async_remote_copy(
            src_ref=held.at[source, chunk_of(c)],
            dst_ref=held.at[source, chunk_of(c)],
            send_sem=sem,
            recv_sem=recv_sem.at[source, c],
            device_id=(group, inst, target),
            device_id_type=MESH,
        )

    def send_meta(e, source):
        return pltpu.make_async_remote_copy(
            src_ref=meta_mine,
            dst_ref=meta_held.at[source],
            send_sem=meta_send.at[e],
            recv_sem=meta_recv.at[source],
            device_id=(group, far, e),
            device_id_type=MESH,
        )

    for c in range(steps):
        compute(c)
        if c == 0:
            pl.semaphore_wait(barrier, n_dp + 1 + len(columns))
        send_far(c).start()
        if c == 0:
            for e in range(n_dp):
                send_meta(e, rank).start()

    def spread(c):
        send_far(c).wait_recv()
        for j, other in enumerate(columns):
            pass_on(c, rank, other, pass_sem.at[j, c]).start()
        pass_on(c, rank, sibling, pass_sem.at[n_y - 1, c]).start()

    def relay(c):
        for j, other in enumerate(columns):
            pass_on(c, other, other, relay_sem.at[j, c]).wait_recv()
            pass_on(c, other, sibling, relay_sem.at[j, c]).start()

    for c in range(steps):
        spread(c)
        if c == 0:
            for d in range(n_dp):
                send_meta(0, d).wait_recv()
            to_smem = pltpu.make_async_copy(meta_held, meta_smem, meta_local)
            to_smem.start()
            to_smem.wait()
        if c > 0:
            relay(c - 1)
    relay(steps - 1)
    for c in range(steps):
        for source in [sibling] + [o // 2 * 2 + 1 - core for o in columns]:
            pass_on(c, source, sibling, pass_sem.at[0, c]).wait_recv()

    for b in range(n_dp):
        page = b * (capacity // BLOCK)
        source, start, count = jnp.int32(0), jnp.int32(0), jnp.int32(0)
        for d in range(n_dp):
            here = meta_smem[d, rank, 2] == page
            source = jnp.where(here, d, source)
            start = jnp.where(here, meta_smem[d, rank, 0], start)
            count = jnp.where(here, meta_smem[d, rank, 1], count)
        out_row = lax.broadcasted_iota(jnp.int32, (capacity, tokens), 0)
        in_row = lax.broadcasted_iota(jnp.int32, (capacity, tokens), 1)
        pick = (in_row == out_row + start) & (out_row < count)
        pick = jnp.where(pick, 1.0, 0.0).astype(jnp.bfloat16)
        left, right = [], []
        for c in range(steps):
            base, rows = packed(first_row[c]), CHUNKS[c]
            left.append(
                jnp.concatenate(
                    [held[source, pl.ds(base + j * rows, rows), :] for j in range(pieces)], axis=1
                )
            )
            both = held[source, pl.ds(base + pieces * rows, rows // 2), :]
            right.append(both[:, :rotary])
            right.append(both[:, rotary:])
        left = jnp.concatenate(left, axis=0)
        right = jnp.concatenate(right, axis=0)
        place = pl.ds(b * capacity, capacity)
        out_ref[place, pl.ds(0, latent)] = jnp.dot(
            pick, left, preferred_element_type=jnp.float32
        ).astype(out_ref.dtype)
        out_ref[place, pl.ds(latent, rotary)] = jnp.dot(
            pick, right, preferred_element_type=jnp.float32
        ).astype(out_ref.dtype)

    for e in range(n_dp):
        send_meta(e, rank).wait_send()
    for c in range(steps):
        send_far(c).wait_send()
        for j, other in enumerate(columns):
            pass_on(c, rank, other, pass_sem.at[j, c]).wait_send()
            pass_on(c, other, sibling, relay_sem.at[j, c]).wait_send()
        pass_on(c, rank, sibling, pass_sem.at[n_y - 1, c]).wait_send()


def on_device(
    n_inst, n_dp, hidden, input_gain, w_latent, latent_norm_gain, req_len, req_dest, req_block
):
    tokens, width = hidden.shape
    lat = w_latent.shape[1]
    latent = latent_norm_gain.shape[0]
    steps = len(CHUNKS)
    n_y = n_dp // 2
    words = tokens * lat // LANES
    meta_rows = max(8, n_dp)
    smem = pl.BlockSpec(memory_space=pltpu.SMEM)
    vmem = pl.BlockSpec(memory_space=pltpu.VMEM)
    hbm = pl.BlockSpec(memory_space=pl.ANY)
    dma = pltpu.SemaphoreType.DMA
    return pl.pallas_call(
        functools.partial(kernel, (n_inst, n_dp)),
        out_shape=jax.ShapeDtypeStruct((2 * tokens, lat), jnp.bfloat16),
        in_specs=[smem, smem, smem, vmem, vmem, hbm, hbm],
        out_specs=vmem,
        scratch_shapes=[
            pltpu.VMEM((tokens, width), jnp.bfloat16),
            pltpu.VMEM((width, lat), jnp.bfloat16),
            pltpu.VMEM((max(CHUNKS), lat), jnp.float32),
            pltpu.VMEM((tokens, LANES), jnp.float32),
            pltpu.VMEM((words, LANES), jnp.bfloat16),
            pltpu.VMEM((n_dp, words, LANES), jnp.bfloat16),
            pltpu.VMEM((meta_rows, LANES), jnp.int32),
            pltpu.VMEM((n_dp, meta_rows, LANES), jnp.int32),
            pltpu.SMEM((n_dp, meta_rows, LANES), jnp.int32),
            dma((steps,)),
            dma((width // KTILE,)),
            dma((steps,)),
            dma((n_y, steps)),
            dma((n_y, steps)),
            dma((n_dp, steps)),
            dma((n_dp,)),
            dma((n_dp,)),
            dma,
        ],
        compiler_params=pltpu.CompilerParams(
            collective_id=0, has_side_effects=True, vmem_limit_bytes=48 * 1024 * 1024
        ),
        cost_estimate=pl.CostEstimate(
            flops=2 * tokens * width * lat,
            bytes_accessed=2 * (tokens * width + width * lat + 2 * tokens * lat),
            transcendentals=tokens * LANES,
        ),
    )(
        req_len,
        req_dest,
        req_block,
        input_gain.reshape(1, width),
        latent_norm_gain.reshape(1, latent),
        hidden,
        w_latent,
    )


def solution(mesh):
    placed = (
        P(("groups", "inst", "dp"), None),
        P(),
        P(),
        P(),
        P(("groups", "inst"), "dp", None),
        P(("groups", "inst"), "dp", None),
        P(("groups", "inst"), "dp", None),
    )
    return jax.shard_map(
        functools.partial(on_device, mesh.shape["inst"], mesh.shape["dp"]),
        mesh=mesh,
        in_specs=placed,
        out_specs=P(("groups", "inst", "dp"), None),
        check_vma=False,
    )
```

time: 114 us -> 59.4 us (0.52)
  waiting for transfers between devices: 62.1 us -> 0 us
  Pallas kernels: 0 us -> 45 us
  starting transfers between devices: 14.1 us -> 0 us
  other arithmetic: 10.7 us -> 0 us
  matrix products: 7.03 us -> 0 us
  blocking collectives: 6.15 us -> 0 us
  local copies, waits for them, and re-layouts: 12.3 us -> 13.9 us
    ppermute x3 -> x0, waiting for transfers between devices: 53.8 us -> none  [from_behind(): return lax.ppermute(block, axis, route)]
    pallas_call x0 -> x1, Pallas kernels: none -> 45 us  [on_device(): pl.pallas_call(functools.partial(kernel, (n_inst, n_dp)), out_shape=jax.S...]
    unnamed x9 -> x11, local copies, waits for them, and re-layouts: 0.4 us -> 12.5 us
    gather x3 -> x0, local copies, waits for them, and re-layouts: 8.7 us -> none  [the longest x2 4.67 us: pack_slots(): jnp.take(cache_rows_out, index.reshape(-1), axis=0)]
    all_to_all x2 -> x0, starting transfers between devices: 8.48 us -> none  [the longest x1 4.29 us: on_device(): lax.all_to_all(slot_len, 'dp', split_axis=0, concat_axis=0, tiled=True)]
    all_to_all x2 -> x0, waiting for transfers between devices: 8.34 us -> none  [the longest x1 8.34 us: on_device(): lax.all_to_all(slots, 'dp', split_axis=0, concat_axis=0, tiled=True)]
    dot_general x1 -> x0, matrix products: 7.03 us -> none  [make_rows(): jnp.dot(normed, w_latent, preferred_element_type=jnp.float32)]
    all_to_all x1 -> x0, blocking collectives: 6.15 us -> none  [on_device(): lax.all_to_all(slot_block, 'dp', split_axis=0, concat_axis=0, tiled=True)]
  transfers between devices with their start and end apart: 5 -> 0, of which waited for: 4 -> 0; matrix products, arithmetic and copies ran while one was open for 17% -> 0% of each run, Pallas kernels for 0% -> 0%
where the time goes in v1:
time: 59.4 us; the launch traced here: 59 us
  Pallas kernels  45 us (76%)
  local copies, waits for them, and re-layouts  13.9 us (23%)
    pallas_call x1, Pallas kernels, on_device(): pl.pallas_call(functools.partial(kernel, (n_inst, n_dp)), out_shape=jax.S...  45 us
    unnamed x11, local copies, waits for them, and re-layouts  12.5 us
    pallas_call x1, local copies, waits for them, and re-layouts, on_device(): pl.pallas_call(functools.partial(kernel, (n_inst, n_dp)), out_shape=jax.S...  1.42 us

profile of v1, /device:TPU:1, one launch (start us, length us, event | category | flops | bytes accessed | tf_op | source)
XLA Modules:
  0.0 59.0 jit_solution(4798024999628416645)
XLA Ops:
  0.0 0.0 copy-start
  0.0 0.0 copy-start.1
  0.0 0.0 copy-start.2
  0.0 0.0 copy-start.3
  0.0 0.0 copy-start.4
  0.0 12.5 %copy.8.w_ref = bf16[7168,576]{1,0:T(8,128)(2,1)} copy(bf16[7168,576]{0,1:T(8,128)(2,1)} %param.9) | data formatting | bytes 16515072 | tf_op args[2]
  12.5 0.0 copy-done
  12.5 0.0 copy-done.1
  12.5 0.0 copy-done.2
  12.5 0.0 copy-done.3
  12.5 0.0 copy-done.4
  12.5 45.0 %shard_map.73 = bf16[1024,576]{1,0:T(8,128)(2,1)S(1)} custom-call(s32[1,1,4]{2,1,0:T(1,128)S(1)} %copy-done.2, s32[1,1,4]{2,1,0:T(1,128)S(1)} %copy-done.3, s32[1,1,4]{2,1,0:T(1,128)S(1)} %copy-done.4, f32[1,7168]{1,0:T(1,128)S(1)} %bitcast.2, f32[1,512]{1,0:T(1,128)S(1)} %bitcast.3, bf16[512,7168]{1,0:T(8,128)(2,1)} %x_ref.1, bf16[7168,576]{1,0:T(8,128)(2,1)} %copy.8.w_ref), custom_call_target="tpu_custom_call" | custom-call | flops 4227858432 | bytes 16777216 | tf_op jit(solution)/shard_map/pallas_call | solution.py:281
  57.6 1.4 %copy.9 = bf16[1024,576]{0,1:T(8,128)(2,1)} copy(bf16[1024,576]{1,0:T(8,128)(2,1)S(1)} %shard_map.73) | data formatting | bytes 2359296 | tf_op jit(solution)/shard_map/pallas_call | solution.py:281
Async XLA Ops:
  0.0 12.5 %copy-start = (f32[7168]{0:T(1024)S(1)}, f32[7168]{0:T(1024)}, u32[]{:S(2)}) copy-start(f32[7168]{0:T(1024)} %param.8) | copy-start | bytes 86020
  0.0 12.5 %copy-start.1 = (f32[512]{0:T(512)S(1)}, f32[512]{0:T(512)}, u32[]{:S(2)}) copy-start(f32[512]{0:T(512)} %param.10) | copy-start | bytes 6148
  0.0 12.5 %copy-start.2 = (s32[1,1,4]{2,1,0:T(1,128)S(1)}, s32[1,1,4]{2,1,0:T(1,128)}, u32[]{:S(2)}) copy-start(s32[1,1,4]{2,1,0:T(1,128)} %len_ref.1) | copy-start | bytes 52
  0.0 12.5 %copy-start.3 = (s32[1,1,4]{2,1,0:T(1,128)S(1)}, s32[1,1,4]{2,1,0:T(1,128)}, u32[]{:S(2)}) copy-start(s32[1,1,4]{2,1,0:T(1,128)} %dest_ref.1) | copy-start | bytes 52
  0.0 12.5 %copy-start.4 = (s32[1,1,4]{2,1,0:T(1,128)S(1)}, s32[1,1,4]{2,1,0:T(1,128)}, u32[]{:S(2)}) copy-start(s32[1,1,4]{2,1,0:T(1,128)} %block_ref.1) | copy-start | bytes 52

commit v2 on v1

v2 whole, which is shorter than its diff:
```python
import functools
import math

import jax
import jax.numpy as jnp
from jax import lax
from jax.experimental import pallas as pl
from jax.experimental.pallas import tpu as pltpu
from jax.sharding import PartitionSpec as P

BLOCK = 64
LANES = 128
MESH = pl.DeviceIdType.MESH
CHUNKS = (128, 128, 256)
SPLIT = 2
KTILE = 1024


def kernel(
    sizes,
    len_ref,
    dest_ref,
    block_ref,
    gain_ref,
    norm_ref,
    x_ref,
    w_ref,
    out_ref,
    x_v,
    w_v,
    acc,
    trig,
    norm,
    mine,
    held,
    meta_mine,
    meta_held,
    meta_smem,
    x_sem,
    w_sem,
    z_sem,
    pass_sem,
    relay_sem,
    recv_sem,
    meta_send,
    meta_recv,
    meta_local,
):
    n_inst, n_dp = sizes
    units, tokens, width = mine.shape[0], x_v.shape[0], x_v.shape[1]
    features = w_ref.shape[0]
    latent = norm_ref.shape[1]
    half = (features - latent) // 2
    capacity = 2 * tokens // n_dp
    n_y = n_dp // 2
    steps = units * SPLIT
    part = features // SPLIT
    first_row = [sum(CHUNKS[:c]) for c in range(len(CHUNKS))]

    group = lax.axis_index("groups")
    inst = lax.axis_index("inst")
    rank = lax.axis_index("dp")
    far = lax.rem(inst + n_inst // 2, n_inst)
    y = rank // 2
    core = lax.rem(rank, 2)
    sibling = y * 2 + 1 - core
    columns = [lax.rem(y + j, n_y) * 2 + core for j in range(1, n_y)]

    w_copies = [
        pltpu.make_async_copy(
            w_ref.at[:, pl.ds(k * KTILE, KTILE)], w_v.at[:, pl.ds(k * KTILE, KTILE)], w_sem.at[k]
        )
        for k in range(width // KTILE)
    ]
    x_copies = [
        pltpu.make_async_copy(
            x_ref.at[pl.ds(first_row[c], CHUNKS[c]), :],
            x_v.at[pl.ds(first_row[c], CHUNKS[c]), :],
            x_sem.at[c],
        )
        for c in range(len(CHUNKS))
    ]
    x_copies[0].start()
    for copy in w_copies:
        copy.start()
    for copy in x_copies[1:]:
        copy.start()

    barrier = pltpu.get_barrier_semaphore()
    for e in range(n_dp):
        pl.semaphore_signal(barrier, inc=1, device_id=(group, far, e), device_id_type=MESH)
    for other in [sibling] + columns:
        pl.semaphore_signal(barrier, inc=1, device_id=(group, inst, other), device_id_type=MESH)

    starts = []
    total = jnp.int32(0)
    for k in range(n_dp):
        starts.append(total)
        total = total + len_ref[0, 0, k]
    row = lax.broadcasted_iota(jnp.int32, meta_mine.shape, 0)
    lane = lax.broadcasted_iota(jnp.int32, meta_mine.shape, 1)
    table = jnp.zeros(meta_mine.shape, jnp.int32)
    for k in range(n_dp):
        entry = jnp.where(
            lane == 0,
            starts[k],
            jnp.where(lane == 1, len_ref[0, 0, k], block_ref[0, 0, k]),
        )
        table = jnp.where(row == dest_ref[0, 0, k], entry, table)
    meta_mine[...] = table

    which = lax.broadcasted_iota(jnp.int32, (half, tokens), 0).astype(jnp.float32)
    inverse = jnp.exp(which * jnp.float32(-math.log(10000.0) / half))
    at = lax.broadcasted_iota(jnp.int32, (half, tokens), 1)
    begin = jnp.zeros((half, tokens), jnp.int32)
    for k in range(1, n_dp):
        begin = jnp.where(at >= starts[k], starts[k], begin)
    angle = (at - begin).astype(jnp.float32) * inverse
    trig[pl.ds(0, half), :] = jnp.cos(angle)
    trig[pl.ds(half, half), :] = jnp.sin(angle)

    norm[...] = jnp.broadcast_to(norm_ref[...], (LANES, latent)).T

    def compute(c):
        rows = CHUNKS[c]
        span = pl.ds(first_row[c], rows)
        x_copies[c].wait()
        squares = jnp.zeros((rows, LANES), jnp.float32)
        for k in range(width // KTILE):
            if c == 0:
                w_copies[k].wait()
            cols = pl.ds(k * KTILE, KTILE)
            values = x_v[span, cols].astype(jnp.float32)
            powers = values * values
            for j in range(KTILE // LANES):
                squares = squares + powers[:, j * LANES : (j + 1) * LANES]
            scaled = (values * gain_ref[:, cols]).astype(jnp.bfloat16)
            product = lax.dot_general(
                w_v[:, cols],
                scaled,
                (((1,), (1,)), ((), ())),
                preferred_element_type=jnp.float32,
            )
            if k == 0:
                acc[:, pl.ds(0, rows)] = product
            else:
                acc[:, pl.ds(0, rows)] += product
        squares = jnp.sum(squares.T, axis=0, keepdims=True)
        scale = lax.rsqrt(squares * (1.0 / width) + 1e-06)
        compressed = acc[pl.ds(0, latent), pl.ds(0, rows)] * scale
        power = jnp.mean(compressed * compressed, axis=0, keepdims=True)
        compressed = compressed * lax.rsqrt(power + 1e-06)
        a = acc[pl.ds(latent, half), pl.ds(0, rows)] * scale
        b = acc[pl.ds(latent + half, half), pl.ds(0, rows)] * scale
        cosine, sine = trig[pl.ds(0, half), span], trig[pl.ds(half, half), span]
        turned = jnp.concatenate([a * cosine - b * sine, a * sine + b * cosine], axis=0)
        for u in range(rows // LANES):
            lanes = slice(u * LANES, (u + 1) * LANES)
            unit = first_row[c] // LANES + u
            mine[unit, pl.ds(0, latent), :] = (compressed[:, lanes] * norm[...]).astype(jnp.bfloat16)
            mine[unit, pl.ds(latent, 2 * half), :] = turned[:, lanes].astype(jnp.bfloat16)

    def rows_of(s):
        return pl.ds((s % SPLIT) * part, part)

    def send_far(s):
        return pltpu.make_async_remote_copy(
            src_ref=mine.at[s // SPLIT, rows_of(s)],
            dst_ref=held.at[rank, s // SPLIT, rows_of(s)],
            send_sem=z_sem.at[s],
            recv_sem=recv_sem.at[rank, s],
            device_id=(group, far, rank),
            device_id_type=MESH,
        )

    def pass_on(c, source, target, sem):
        return pltpu.make_async_remote_copy(
            src_ref=held.at[source, c // SPLIT, rows_of(c)],
            dst_ref=held.at[source, c // SPLIT, rows_of(c)],
            send_sem=sem,
            recv_sem=recv_sem.at[source, c],
            device_id=(group, inst, target),
            device_id_type=MESH,
        )

    def send_meta(e, source):
        return pltpu.make_async_remote_copy(
            src_ref=meta_mine,
            dst_ref=meta_held.at[source],
            send_sem=meta_send.at[e],
            recv_sem=meta_recv.at[source],
            device_id=(group, far, e),
            device_id_type=MESH,
        )

    for c in range(len(CHUNKS)):
        compute(c)
        if c == 0:
            pl.semaphore_wait(barrier, n_dp + 1 + len(columns))
        for s in range(CHUNKS[c] // LANES * SPLIT):
            send_far(first_row[c] // LANES * SPLIT + s).start()
        if c == 0:
            for e in range(n_dp):
                send_meta(e, rank).start()

    def spread(c):
        send_far(c).wait_recv()
        for j, other in enumerate(columns):
            pass_on(c, rank, other, pass_sem.at[j, c]).start()
        pass_on(c, rank, sibling, pass_sem.at[n_y - 1, c]).start()

    def relay(c):
        for j, other in enumerate(columns):
            pass_on(c, other, other, relay_sem.at[j, c]).wait_recv()
            pass_on(c, other, sibling, relay_sem.at[j, c]).start()

    for c in range(steps):
        spread(c)
        if c == 0:
            for d in range(n_dp):
                send_meta(0, d).wait_recv()
            to_smem = pltpu.make_async_copy(meta_held, meta_smem, meta_local)
            to_smem.start()
            to_smem.wait()
        if c > 0:
            relay(c - 1)
    relay(steps - 1)
    for c in range(steps):
        for source in [sibling] + [o // 2 * 2 + 1 - core for o in columns]:
            pass_on(c, source, sibling, pass_sem.at[0, c]).wait_recv()

    together = max(1, LANES // capacity)
    for first in range(0, n_dp, together):
        blocks = []
        for b in range(first, first + together):
            page = b * (capacity // BLOCK)
            source, start, count = jnp.int32(0), jnp.int32(0), jnp.int32(0)
            for d in range(n_dp):
                here = meta_smem[d, rank, 2] == page
                source = jnp.where(here, d, source)
                start = jnp.where(here, meta_smem[d, rank, 0], start)
                count = jnp.where(here, meta_smem[d, rank, 1], count)
            in_row = lax.broadcasted_iota(jnp.int32, (tokens, capacity), 0)
            out_row = lax.broadcasted_iota(jnp.int32, (tokens, capacity), 1)
            pick = (in_row == out_row + start) & (out_row < count)
            pick = jnp.where(pick, 1.0, 0.0).astype(jnp.bfloat16)
            rows = jnp.concatenate([held[source, u] for u in range(units)], axis=1)
            blocks.append(jnp.dot(rows, pick, preferred_element_type=jnp.float32))
        block = blocks[0] if together == 1 else jnp.concatenate(blocks, axis=1)
        out_ref[:, pl.ds(first * capacity, together * capacity)] = block.astype(out_ref.dtype)

    for e in range(n_dp):
        send_meta(e, rank).wait_send()
    for c in range(steps):
        send_far(c).wait_send()
        for j, other in enumerate(columns):
            pass_on(c, rank, other, pass_sem.at[j, c]).wait_send()
            pass_on(c, other, sibling, relay_sem.at[j, c]).wait_send()
        pass_on(c, rank, sibling, pass_sem.at[n_y - 1, c]).wait_send()


def on_device(
    n_inst, n_dp, hidden, input_gain, w_latent, latent_norm_gain, req_len, req_dest, req_block
):
    tokens, width = hidden.shape
    lat = w_latent.shape[1]
    latent = latent_norm_gain.shape[0]
    units = tokens // LANES
    steps = units * SPLIT
    n_y = n_dp // 2
    meta_rows = max(8, n_dp)
    smem = pl.BlockSpec(memory_space=pltpu.SMEM)
    vmem = pl.BlockSpec(memory_space=pltpu.VMEM)
    hbm = pl.BlockSpec(memory_space=pl.ANY)
    dma = pltpu.SemaphoreType.DMA
    placed = pl.pallas_call(
        functools.partial(kernel, (n_inst, n_dp)),
        out_shape=jax.ShapeDtypeStruct((lat, 2 * tokens), jnp.bfloat16),
        in_specs=[smem, smem, smem, vmem, vmem, hbm, hbm],
        out_specs=vmem,
        scratch_shapes=[
            pltpu.VMEM((tokens, width), jnp.bfloat16),
            pltpu.VMEM((lat, width), jnp.bfloat16),
            pltpu.VMEM((lat, max(CHUNKS)), jnp.float32),
            pltpu.VMEM((lat - latent, tokens), jnp.float32),
            pltpu.VMEM((latent, LANES), jnp.float32),
            pltpu.VMEM((units, lat, LANES), jnp.bfloat16),
            pltpu.VMEM((n_dp, units, lat, LANES), jnp.bfloat16),
            pltpu.VMEM((meta_rows, LANES), jnp.int32),
            pltpu.VMEM((n_dp, meta_rows, LANES), jnp.int32),
            pltpu.SMEM((n_dp, meta_rows, LANES), jnp.int32),
            dma((len(CHUNKS),)),
            dma((width // KTILE,)),
            dma((steps,)),
            dma((n_y, steps)),
            dma((n_y, steps)),
            dma((n_dp, steps)),
            dma((n_dp,)),
            dma((n_dp,)),
            dma,
        ],
        compiler_params=pltpu.CompilerParams(
            collective_id=0, has_side_effects=True, vmem_limit_bytes=48 * 1024 * 1024
        ),
        cost_estimate=pl.CostEstimate(
            flops=2 * tokens * width * lat,
            bytes_accessed=2 * (tokens * width + width * lat + 2 * tokens * lat),
            transcendentals=tokens * LANES,
        ),
    )(
        req_len,
        req_dest,
        req_block,
        input_gain.reshape(1, width),
        latent_norm_gain.reshape(1, latent),
        hidden,
        w_latent.T,
    )
    return placed.T


def solution(mesh):
    placed = (
        P(("groups", "inst", "dp"), None),
        P(),
        P(),
        P(),
        P(("groups", "inst"), "dp", None),
        P(("groups", "inst"), "dp", None),
        P(("groups", "inst"), "dp", None),
    )
    return jax.shard_map(
        functools.partial(on_device, mesh.shape["inst"], mesh.shape["dp"]),
        mesh=mesh,
        in_specs=placed,
        out_specs=P(("groups", "inst", "dp"), None),
        check_vma=False,
    )
```

time: 59.4 us -> 54.3 us (0.914)
  local copies, waits for them, and re-layouts: 13.9 us -> 4.41 us
  Pallas kernels: 45 us -> 49.7 us
    unnamed x11, local copies, waits for them, and re-layouts: 12.5 us -> 4.41 us
    pallas_call x1, Pallas kernels: 45 us -> 49.7 us  [on_device(): pl.pallas_call(functools.partial(kernel, (n_inst, n_dp)), out_shape=jax.S...]
    pallas_call x1 -> x0, local copies, waits for them, and re-layouts: 1.42 us -> none  [on_device(): pl.pallas_call(functools.partial(kernel, (n_inst, n_dp)), out_shape=jax.S...]
where the time goes in v2:
time: 54.3 us; the launch traced here: 54.1 us
  Pallas kernels  49.7 us (92%)
  local copies, waits for them, and re-layouts  4.41 us (8%)
    pallas_call x1, Pallas kernels, on_device(): pl.pallas_call(functools.partial(kernel, (n_inst, n_dp)), out_shape=jax.S...  49.7 us
    unnamed x11, local copies, waits for them, and re-layouts  4.41 us

profile of v2, /device:TPU:1, one launch (start us, length us, event | category | flops | bytes accessed | tf_op | source)
XLA Modules:
  0.0 54.1 jit_solution(17636739110916572687)
XLA Ops:
  0.0 0.0 copy-start
  0.0 0.7 %copy-done = f32[7168]{0:T(1024)S(1)} copy-done((f32[7168]{0:T(1024)S(1)}, f32[7168]{0:T(1024)}, u32[]{:S(2)}) %copy-start) | copy-done | bytes 28696
  0.7 0.0 copy-start.1
  0.8 0.7 %copy-done.1 = f32[512]{0:T(512)S(1)} copy-done((f32[512]{0:T(512)S(1)}, f32[512]{0:T(512)}, u32[]{:S(2)}) %copy-start.1) | copy-done | bytes 2072
  1.4 0.0 copy-start.2
  1.4 0.7 %copy-done.2 = s32[1,1,4]{2,1,0:T(1,128)S(1)} copy-done((s32[1,1,4]{2,1,0:T(1,128)S(1)}, s32[1,1,4]{2,1,0:T(1,128)}, u32[]{:S(2)}) %copy-start.2) | copy-done | bytes 40
  2.1 0.0 copy-start.3
  2.1 0.7 %copy-done.3 = s32[1,1,4]{2,1,0:T(1,128)S(1)} copy-done((s32[1,1,4]{2,1,0:T(1,128)S(1)}, s32[1,1,4]{2,1,0:T(1,128)}, u32[]{:S(2)}) %copy-start.3) | copy-done | bytes 40
  2.7 0.0 copy-start.4
  2.7 0.7 %copy-done.4 = s32[1,1,4]{2,1,0:T(1,128)S(1)} copy-done((s32[1,1,4]{2,1,0:T(1,128)S(1)}, s32[1,1,4]{2,1,0:T(1,128)}, u32[]{:S(2)}) %copy-start.4) | copy-done | bytes 40
  3.4 49.7 %shard_map.73 = bf16[576,1024]{1,0:T(8,128)(2,1)S(1)} custom-call(s32[1,1,4]{2,1,0:T(1,128)S(1)} %copy-done.2, s32[1,1,4]{2,1,0:T(1,128)S(1)} %copy-done.3, s32[1,1,4]{2,1,0:T(1,128)S(1)} %copy-done.4, f32[1,7168]{1,0:T(1,128)S(1)} %bitcast.5, f32[1,512]{1,0:T(1,128)S(1)} %bitcast.6, bf16[512,7168]{1,0:T(8,128)(2,1)} %x_ref.1, bf16[576,7168]{1,0:T(8,128)(2,1)} %bitcast.7), custom_call_target="tpu_custom_call" | custom-call | flops 4227858432 | bytes 16777216 | tf_op jit(solution)/shard_map/pallas_call | solution.py:276
  53.1 1.0 %copy.9 = bf16[1024,576]{0,1:T(8,128)(2,1)} copy(bf16[1024,576]{0,1:T(8,128)(2,1)S(1)} %bitcast.4) | data formatting | bytes 2359296
Async XLA Ops:
  0.0 0.7 %copy-start = (f32[7168]{0:T(1024)S(1)}, f32[7168]{0:T(1024)}, u32[]{:S(2)}) copy-start(f32[7168]{0:T(1024)} %param.8) | copy-start | bytes 86020
  0.7 0.7 %copy-start.1 = (f32[512]{0:T(512)S(1)}, f32[512]{0:T(512)}, u32[]{:S(2)}) copy-start(f32[512]{0:T(512)} %param.10) | copy-start | bytes 6148
  1.4 0.7 %copy-start.2 = (s32[1,1,4]{2,1,0:T(1,128)S(1)}, s32[1,1,4]{2,1,0:T(1,128)}, u32[]{:S(2)}) copy-start(s32[1,1,4]{2,1,0:T(1,128)} %len_ref.1) | copy-start | bytes 52
  2.1 0.7 %copy-start.3 = (s32[1,1,4]{2,1,0:T(1,128)S(1)}, s32[1,1,4]{2,1,0:T(1,128)}, u32[]{:S(2)}) copy-start(s32[1,1,4]{2,1,0:T(1,128)} %dest_ref.1) | copy-start | bytes 52
  2.7 0.7 %copy-start.4 = (s32[1,1,4]{2,1,0:T(1,128)S(1)}, s32[1,1,4]{2,1,0:T(1,128)}, u32[]{:S(2)}) copy-start(s32[1,1,4]{2,1,0:T(1,128)} %block_ref.1) | copy-start | bytes 52

commit v3 on v2

--- a/solution.py
+++ b/solution.py
@@ -11,8 +11,7 @@
 BLOCK = 64
 LANES = 128
 MESH = pl.DeviceIdType.MESH
-CHUNKS = (128, 128, 256)
-SPLIT = 2
+CHUNKS = (128, 128, 128, 128)
 KTILE = 1024
 
 
@@ -53,8 +52,7 @@
     half = (features - latent) // 2
     capacity = 2 * tokens // n_dp
     n_y = n_dp // 2
-    steps = units * SPLIT
-    part = features // SPLIT
+    steps = len(CHUNKS)
     first_row = [sum(CHUNKS[:c]) for c in range(len(CHUNKS))]
 
     group = lax.axis_index("groups")
@@ -160,13 +158,13 @@
             mine[unit, pl.ds(0, latent), :] = (compressed[:, lanes] * norm[...]).astype(jnp.bfloat16)
             mine[unit, pl.ds(latent, 2 * half), :] = turned[:, lanes].astype(jnp.bfloat16)
 
-    def rows_of(s):
-        return pl.ds((s % SPLIT) * part, part)
+    def chunk_of(c):
+        return pl.ds(first_row[c] // LANES, CHUNKS[c] // LANES)
 
     def send_far(s):
         return pltpu.make_async_remote_copy(
-            src_ref=mine.at[s // SPLIT, rows_of(s)],
-            dst_ref=held.at[rank, s // SPLIT, rows_of(s)],
+            src_ref=mine.at[chunk_of(s)],
+            dst_ref=held.at[rank, chunk_of(s)],
             send_sem=z_sem.at[s],
             recv_sem=recv_sem.at[rank, s],
             device_id=(group, far, rank),
@@ -175,8 +173,8 @@
 
     def pass_on(c, source, target, sem):
         return pltpu.make_async_remote_copy(
-            src_ref=held.at[source, c // SPLIT, rows_of(c)],
-            dst_ref=held.at[source, c // SPLIT, rows_of(c)],
+            src_ref=held.at[source, chunk_of(c)],
+            dst_ref=held.at[source, chunk_of(c)],
             send_sem=sem,
             recv_sem=recv_sem.at[source, c],
             device_id=(group, inst, target),
@@ -197,8 +195,7 @@
         compute(c)
         if c == 0:
             pl.semaphore_wait(barrier, n_dp + 1 + len(columns))
-        for s in range(CHUNKS[c] // LANES * SPLIT):
-            send_far(first_row[c] // LANES * SPLIT + s).start()
+        send_far(c).start()
         if c == 0:
             for e in range(n_dp):
                 send_meta(e, rank).start()
@@ -266,7 +263,7 @@
     lat = w_latent.shape[1]
     latent = latent_norm_gain.shape[0]
     units = tokens // LANES
-    steps = units * SPLIT
+    steps = len(CHUNKS)
     n_y = n_dp // 2
     meta_rows = max(8, n_dp)
     smem = pl.BlockSpec(memory_space=pltpu.SMEM)

time: 54.3 us -> 50.9 us (0.937)
  Pallas kernels: 49.7 us -> 46.2 us
    pallas_call x1, Pallas kernels: 49.7 us -> 46.2 us  [on_device(): pl.pallas_call(functools.partial(kernel, (n_inst, n_dp)), out_shape=jax.S...]
where the time goes in v3:
time: 50.9 us; the launch traced here: 50.6 us
  Pallas kernels  46.2 us (91%)
  local copies, waits for them, and re-layouts  4.41 us (9%)
    pallas_call x1, Pallas kernels, on_device(): pl.pallas_call(functools.partial(kernel, (n_inst, n_dp)), out_shape=jax.S...  46.2 us
    unnamed x11, local copies, waits for them, and re-layouts  4.41 us

profile of v3, /device:TPU:1, one launch (start us, length us, event | category | flops | bytes accessed | tf_op | source)
XLA Modules:
  0.0 50.6 jit_solution(6050498061824719129)
XLA Ops:
  0.0 0.0 copy-start
  0.0 0.7 %copy-done = f32[7168]{0:T(1024)S(1)} copy-done((f32[7168]{0:T(1024)S(1)}, f32[7168]{0:T(1024)}, u32[]{:S(2)}) %copy-start) | copy-done | bytes 28696
  0.7 0.0 copy-start.1
  0.8 0.7 %copy-done.1 = f32[512]{0:T(512)S(1)} copy-done((f32[512]{0:T(512)S(1)}, f32[512]{0:T(512)}, u32[]{:S(2)}) %copy-start.1) | copy-done | bytes 2072
  1.4 0.0 copy-start.2
  1.4 0.7 %copy-done.2 = s32[1,1,4]{2,1,0:T(1,128)S(1)} copy-done((s32[1,1,4]{2,1,0:T(1,128)S(1)}, s32[1,1,4]{2,1,0:T(1,128)}, u32[]{:S(2)}) %copy-start.2) | copy-done | bytes 40
  2.1 0.0 copy-start.3
  2.1 0.7 %copy-done.3 = s32[1,1,4]{2,1,0:T(1,128)S(1)} copy-done((s32[1,1,4]{2,1,0:T(1,128)S(1)}, s32[1,1,4]{2,1,0:T(1,128)}, u32[]{:S(2)}) %copy-start.3) | copy-done | bytes 40
  2.7 0.0 copy-start.4
  2.7 0.7 %copy-done.4 = s32[1,1,4]{2,1,0:T(1,128)S(1)} copy-done((s32[1,1,4]{2,1,0:T(1,128)S(1)}, s32[1,1,4]{2,1,0:T(1,128)}, u32[]{:S(2)}) %copy-start.4) | copy-done | bytes 40
  3.4 46.2 %shard_map.73 = bf16[576,1024]{1,0:T(8,128)(2,1)S(1)} custom-call(s32[1,1,4]{2,1,0:T(1,128)S(1)} %copy-done.2, s32[1,1,4]{2,1,0:T(1,128)S(1)} %copy-done.3, s32[1,1,4]{2,1,0:T(1,128)S(1)} %copy-done.4, f32[1,7168]{1,0:T(1,128)S(1)} %bitcast.5, f32[1,512]{1,0:T(1,128)S(1)} %bitcast.6, bf16[512,7168]{1,0:T(8,128)(2,1)} %x_ref.1, bf16[576,7168]{1,0:T(8,128)(2,1)} %bitcast.7), custom_call_target="tpu_custom_call" | custom-call | flops 4227858432 | bytes 16777216 | tf_op jit(solution)/shard_map/pallas_call | solution.py:273
  49.6 1.0 %copy.9 = bf16[1024,576]{0,1:T(8,128)(2,1)} copy(bf16[1024,576]{0,1:T(8,128)(2,1)S(1)} %bitcast.4) | data formatting | bytes 2359296
Async XLA Ops:
  0.0 0.7 %copy-start = (f32[7168]{0:T(1024)S(1)}, f32[7168]{0:T(1024)}, u32[]{:S(2)}) copy-start(f32[7168]{0:T(1024)} %param.8) | copy-start | bytes 86020
  0.7 0.7 %copy-start.1 = (f32[512]{0:T(512)S(1)}, f32[512]{0:T(512)}, u32[]{:S(2)}) copy-start(f32[512]{0:T(512)} %param.10) | copy-start | bytes 6148
  1.4 0.7 %copy-start.2 = (s32[1,1,4]{2,1,0:T(1,128)S(1)}, s32[1,1,4]{2,1,0:T(1,128)}, u32[]{:S(2)}) copy-start(s32[1,1,4]{2,1,0:T(1,128)} %len_ref.1) | copy-start | bytes 52
  2.1 0.7 %copy-start.3 = (s32[1,1,4]{2,1,0:T(1,128)S(1)}, s32[1,1,4]{2,1,0:T(1,128)}, u32[]{:S(2)}) copy-start(s32[1,1,4]{2,1,0:T(1,128)} %dest_ref.1) | copy-start | bytes 52
  2.7 0.7 %copy-start.4 = (s32[1,1,4]{2,1,0:T(1,128)S(1)}, s32[1,1,4]{2,1,0:T(1,128)}, u32[]{:S(2)}) copy-start(s32[1,1,4]{2,1,0:T(1,128)} %block_ref.1) | copy-start | bytes 52

commit v4 on v3

--- a/solution.py
+++ b/solution.py
@@ -12,7 +12,7 @@
 LANES = 128
 MESH = pl.DeviceIdType.MESH
 CHUNKS = (128, 128, 128, 128)
-KTILE = 1024
+KTILE = 1792
 
 
 def kernel(

time: 50.9 us -> 50.3 us (0.988)
  Pallas kernels: 46.2 us -> 45.6 us
    pallas_call x1, Pallas kernels: 46.2 us -> 45.6 us  [on_device(): pl.pallas_call(functools.partial(kernel, (n_inst, n_dp)), out_shape=jax.S...]
where the time goes in v4:
time: 50.3 us; the launch traced here: 50 us
  Pallas kernels  45.6 us (91%)
  local copies, waits for them, and re-layouts  4.41 us (9%)
    pallas_call x1, Pallas kernels, on_device(): pl.pallas_call(functools.partial(kernel, (n_inst, n_dp)), out_shape=jax.S...  45.6 us
    unnamed x11, local copies, waits for them, and re-layouts  4.41 us

profile of v4, /device:TPU:1, one launch (start us, length us, event | category | flops | bytes accessed | tf_op | source)
XLA Modules:
  0.0 50.0 jit_solution(2831688808996057300)
XLA Ops:
  0.0 0.0 copy-start
  0.0 0.7 %copy-done = f32[7168]{0:T(1024)S(1)} copy-done((f32[7168]{0:T(1024)S(1)}, f32[7168]{0:T(1024)}, u32[]{:S(2)}) %copy-start) | copy-done | bytes 28696
  0.7 0.0 copy-start.1
  0.8 0.7 %copy-done.1 = f32[512]{0:T(512)S(1)} copy-done((f32[512]{0:T(512)S(1)}, f32[512]{0:T(512)}, u32[]{:S(2)}) %copy-start.1) | copy-done | bytes 2072
  1.4 0.0 copy-start.2
  1.4 0.7 %copy-done.2 = s32[1,1,4]{2,1,0:T(1,128)S(1)} copy-done((s32[1,1,4]{2,1,0:T(1,128)S(1)}, s32[1,1,4]{2,1,0:T(1,128)}, u32[]{:S(2)}) %copy-start.2) | copy-done | bytes 40
  2.1 0.0 copy-start.3
  2.1 0.7 %copy-done.3 = s32[1,1,4]{2,1,0:T(1,128)S(1)} copy-done((s32[1,1,4]{2,1,0:T(1,128)S(1)}, s32[1,1,4]{2,1,0:T(1,128)}, u32[]{:S(2)}) %copy-start.3) | copy-done | bytes 40
  2.7 0.0 copy-start.4
  2.7 0.7 %copy-done.4 = s32[1,1,4]{2,1,0:T(1,128)S(1)} copy-done((s32[1,1,4]{2,1,0:T(1,128)S(1)}, s32[1,1,4]{2,1,0:T(1,128)}, u32[]{:S(2)}) %copy-start.4) | copy-done | bytes 40
  3.4 45.6 %shard_map.73 = bf16[576,1024]{1,0:T(8,128)(2,1)S(1)} custom-call(s32[1,1,4]{2,1,0:T(1,128)S(1)} %copy-done.2, s32[1,1,4]{2,1,0:T(1,128)S(1)} %copy-done.3, s32[1,1,4]{2,1,0:T(1,128)S(1)} %copy-done.4, f32[1,7168]{1,0:T(1,128)S(1)} %bitcast.5, f32[1,512]{1,0:T(1,128)S(1)} %bitcast.6, bf16[512,7168]{1,0:T(8,128)(2,1)} %x_ref.1, bf16[576,7168]{1,0:T(8,128)(2,1)} %bitcast.7), custom_call_target="tpu_custom_call" | custom-call | flops 4227858432 | bytes 16777216 | tf_op jit(solution)/shard_map/pallas_call | solution.py:273
  49.0 1.0 %copy.9 = bf16[1024,576]{0,1:T(8,128)(2,1)} copy(bf16[1024,576]{0,1:T(8,128)(2,1)S(1)} %bitcast.4) | data formatting | bytes 2359296
Async XLA Ops:
  0.0 0.7 %copy-start = (f32[7168]{0:T(1024)S(1)}, f32[7168]{0:T(1024)}, u32[]{:S(2)}) copy-start(f32[7168]{0:T(1024)} %param.8) | copy-start | bytes 86020
  0.7 0.7 %copy-start.1 = (f32[512]{0:T(512)S(1)}, f32[512]{0:T(512)}, u32[]{:S(2)}) copy-start(f32[512]{0:T(512)} %param.10) | copy-start | bytes 6148
  1.4 0.7 %copy-start.2 = (s32[1,1,4]{2,1,0:T(1,128)S(1)}, s32[1,1,4]{2,1,0:T(1,128)}, u32[]{:S(2)}) copy-start(s32[1,1,4]{2,1,0:T(1,128)} %len_ref.1) | copy-start | bytes 52
  2.1 0.7 %copy-start.3 = (s32[1,1,4]{2,1,0:T(1,128)S(1)}, s32[1,1,4]{2,1,0:T(1,128)}, u32[]{:S(2)}) copy-start(s32[1,1,4]{2,1,0:T(1,128)} %dest_ref.1) | copy-start | bytes 52
  2.7 0.7 %copy-start.4 = (s32[1,1,4]{2,1,0:T(1,128)S(1)}, s32[1,1,4]{2,1,0:T(1,128)}, u32[]{:S(2)}) copy-start(s32[1,1,4]{2,1,0:T(1,128)} %block_ref.1) | copy-start | bytes 52
